TPU v7x, 1024 devices: a whole 4x4x32 slice. The times are simulated.
1024 devices in a mesh: wide: 256 (over z, y, x_lo), narrow: 4 (over x_hi, core).
Axes of the slice: x: 4 (x_hi: 2, x_lo: 2; x = x_hi * 2 + x_lo), y: 4, z: 32, core: 2. Of those that a mesh axis runs over, the one named last changes fastest.
Arguments:
- chi_in: float32 [40960, 2048], P('wide', 'narrow'), may hold values from -6 to 6
- val_orb: float32 [40960, 4096], P(('wide', 'narrow')), may hold values from -4 to 4
- cond_orb: float32 [40960, 4096], P(('wide', 'narrow')), may hold values from -4 to 4
- e_val: float32 [4096], replicated, may hold values from -12 to -0.5
- e_cond: float32 [4096], replicated, may hold values from 0.5 to 12
- pair_val: int32 [1, 512], replicated, may hold values from 0 to 4095
- pair_cond: int32 [1, 512], replicated, may hold values from 0 to 4095
Outputs:
- chi_out: float32 [40960, 2048], P('wide', 'narrow')
All inputs are finite; a program needn't handle non-finite values.
Results may differ from a plain program's by a relative error of at most 0.0001.
Values sent between devices are 32-bit elements; how exact they have to be, the bound alone decides.
A program may use at most 32 MiB of HBM per device.

v0:
```python
import jax
import jax.numpy as jnp
from jax import lax
from jax.sharding import PartitionSpec as P

SLAB_DEV = 8


def shards(chi_in, val_orb, cond_orb, e_val, e_cond, pair_val, pair_cond):
    narrow_pos = lax.axis_index("narrow")
    row_sub = SLAB_DEV // lax.axis_size("narrow")
    weight = 1.0 / (e_cond[pair_cond] - e_val[pair_val])
    dens_local = val_orb[:, pair_val] * cond_orb[:, pair_cond]
    columns = lax.all_gather(dens_local, "narrow", axis=0, tiled=True)
    weighted = columns * weight[None, :, :]
    pieces = lax.dynamic_slice_in_dim(columns, narrow_pos * row_sub, row_sub, 0)
    block_cols = weighted[:, 0, :]
    return chi_in + jnp.dot(
        block_cols,
        lax.all_gather(pieces[:, 0, :], "wide", axis=0, tiled=True).T,
        precision=lax.Precision.HIGHEST,
        preferred_element_type=jnp.float32,
    )


def solution(mesh):
    placed = (
        P("wide", "narrow"),
        P(("wide", "narrow"), None),
        P(("wide", "narrow"), None),
        P(),
        P(),
        P(),
        P(),
    )
    return jax.shard_map(
        shards, mesh=mesh, in_specs=placed, out_specs=P("wide", "narrow"), check_vma=False
    )
```

profile of v0, /device:TPU:6, one launch (start us, length us, event | category | flops | bytes accessed | tf_op | source)
XLA Modules:
  0.0 922.8 jit_solution(12631795768366566849)
XLA Ops:
  6.5 0.0 copy-start
  6.5 0.0 copy-start.2
  6.5 0.0 all-gather.6.cloned.1.call-start
  6.5 0.8 compare_select_fusion.1
  7.3 0.7 compare_select_fusion
  8.0 3.1 copy.15
  11.1 0.0 copy-done.2
  11.1 0.6 copy.16
  11.7 2.6 gather_fusion
  14.3 0.0 copy-start.1
  14.3 1.0 gather_fusion.1
  15.4 0.1 copy.17
  15.5 7.5 all-gather.1
  23.0 0.6 dynamic-slice_bitcast_fusion
  23.6 0.0 all-gather.6.cloned.1.call-update
  23.6 0.0 copy-done
  23.6 3.1 gather_fusion.3
  26.7 0.0 copy-done.1
  26.8 0.0 copy-start.3
  26.8 3.1 gather_fusion.2
  29.9 882.2 %all-gather.6.cloned.1.call-done = f32[256,2,512]{2,1,0:T(2,128)} async-done(((f32[1,2,512]{2,1,0:T(2,128)}), f32[256,2,512]{2,1,0:T(2,128)}) %all-gather.6.cloned.1.call-update) | async-done | bytes 1048592 | tf_op jit(solution)/shard_map/all_gather | solution.py:20
  912.1 1.9 reshape.78
  914.0 0.0 copy-done.3
  914.0 1.9 convolution_add_fusion
  (4 shorter events, 0.1 us)
Async XLA Ops:
  6.5 17.0 %copy-start = (f32[4096]{0:T(1024)S(1)}, f32[4096]{0:T(1024)}, u32[]{:S(2)}) copy-start(f32[4096]{0:T(1024)} %param.10) | copy-start | bytes 49156
  6.5 4.5 copy-start.2
  6.5 905.5 %all-gather.6.cloned.1.call-start = ((), (), s32[]{:S(2)}) async-start(), calls=%async_computation | async-start | bytes 1052672 | tf_op jit(solution)/shard_map/all_gather | solution.py:20
  14.3 12.5 %copy-start.1 = (f32[4096]{0:T(1024)S(1)}, f32[4096]{0:T(1024)}, u32[]{:S(2)}) copy-start(f32[4096]{0:T(1024)} %param.11) | copy-start | bytes 49156
  26.8 887.3 %copy-start.3 = (f32[160,512]{1,0:T(8,128)S(1)}, f32[160,512]{1,0:T(8,128)}, u32[]{:S(2)}) copy-start(f32[160,512]{1,0:T(8,128)} %param.7) | copy-start | bytes 983044
Sparse Core Ops, SparseCore 0:
  23.7 888.3 all-gather.5
where the time goes:
time: 924 us; the launch traced here: 923 us
  waiting for transfers between devices  882 us (95%)
  local copies, waits for them, and re-layouts  16.3 us (2%)
  between operations  13.5 us (1%)
    all_gather x1, waiting for transfers between devices, shards(): lax.all_gather(pieces[:, 0, :], 'wide', axis=0, tiled=True)  882 us
  transfers between devices with their start and end apart: 1, of which 1 were waited for; matrix products, arithmetic and copies ran while one was open for 1% of the time, Pallas kernels for 0%

commit v1 on v0

v1 whole, which is shorter than its diff:
```python
import functools

import jax
import jax.numpy as jnp
from jax import lax
from jax.experimental import pallas as pl
from jax.experimental.pallas import tpu as pltpu
from jax.sharding import PartitionSpec as P

MESH = pl.DeviceIdType.MESH
LANES = 128
NY = 4
NX = 2
Z_ORDER = (1, 2, 3, 8, 4, 5, 6, 7)


def kernel(
    n_wide, n_narrow, pairs, reach,
    pv_ref, pc_ref, ev_ref, ec_ref, val_ref, cond_ref, chi_ref,
    out_ref,
    pv, pc, ev, ec, vbuf, cbuf, chi, stage, slab, cols,
    in_sems, x_send, x_recv, col_send, col_recv, z_send, z_recv, far_recv, y_send, y_recv,
):
    me_w = lax.axis_index("wide")
    me_n = lax.axis_index("narrow")
    nz = n_wide // (NY * NX)
    z, y, xl = me_w // (NY * NX), (me_w // NX) % NY, me_w % NX
    groups = pairs // LANES
    unit = 2 * groups
    pair_unit = unit * NX
    points = vbuf.shape[0]
    n_x = NX * n_narrow - 1

    def wide_of(zz, yy, xx):
        return (zz * NY + yy) * NX + xx

    def dev(w, n):
        return {"wide": w, "narrow": n}

    def shift_z(dz):
        return lax.rem(z + dz + nz, nz)

    def shift_y(dy):
        return lax.rem(y + dy + NY, NY)

    small = [
        pltpu.make_async_copy(s, d, in_sems.at[i])
        for i, (s, d) in enumerate([(pv_ref, pv), (pc_ref, pc), (ev_ref, ev), (ec_ref, ec)])
    ]
    heads = [
        pltpu.make_async_copy(s.at[pl.ds(0, 8)], d.at[pl.ds(0, 8)], in_sems.at[4 + i])
        for i, (s, d) in enumerate([(val_ref, vbuf), (cond_ref, cbuf)])
    ]
    rests = [
        pltpu.make_async_copy(
            s.at[pl.ds(8, points - 8)], d.at[pl.ds(8, points - 8)], in_sems.at[6 + i]
        )
        for i, (s, d) in enumerate([(val_ref, vbuf), (cond_ref, cbuf)])
    ]
    chi_load = pltpu.make_async_copy(chi_ref, chi, in_sems.at[8])
    for c in small + heads + rests + [chi_load]:
        c.start()

    barrier = pltpu.get_barrier_semaphore()

    def greet(w, n):
        pl.semaphore_signal(barrier, inc=1, device_id=dev(w, n), device_id_type=MESH)

    for src in range(NX):
        @pl.when(jnp.logical_or(me_n != 0, xl != src))
        def _():
            greet(wide_of(z, y, src), 0)
    for k in range(1, n_narrow):
        greet(me_w, lax.rem(me_n + k, n_narrow))
    for dy in (1, 3, 2):
        greet(wide_of(z, shift_y(dy), xl), me_n)
    for dz in range(1, reach + 1):
        greet(wide_of(shift_z(dz), y, xl), me_n)
        greet(wide_of(shift_z(-dz), y, xl), me_n)
    always = (n_narrow - 1) + 3 + 2 * reach

    for c in small:
        c.wait()
    for c in heads:
        c.wait()

    def split(ref, a):
        index = jnp.broadcast_to(ref[0:1, a * LANES:(a + 1) * LANES], (8, LANES))
        return index & (LANES - 1), index >> 7

    idx_v = [split(pv, a) for a in range(groups)]
    idx_c = [split(pc, a) for a in range(groups)]
    chunks = vbuf.shape[1] // LANES

    def pick(load_v, load_c):
        def body(c, acc):
            rows_v, rows_c = load_v(c), load_c(c)
            new = []
            for a in range(groups):
                for rows, (lo, hi), old in (
                    (rows_v, idx_v[a], acc[2 * a]),
                    (rows_c, idx_c[a], acc[2 * a + 1]),
                ):
                    got = jnp.take_along_axis(rows, lo, axis=1, mode="promise_in_bounds")
                    new.append(jnp.where(hi == c, got, old))
            return tuple(new)

        zero = jnp.zeros((8, LANES), jnp.float32)
        return lax.fori_loop(0, chunks, body, (zero,) * (2 * groups))

    def density(start):
        def load(ref):
            return lambda c: ref[
                pl.ds(start, 8), pl.ds(pl.multiple_of(c * LANES, LANES), LANES)
            ]

        got = pick(load(vbuf), load(cbuf))
        return [got[2 * a] * got[2 * a + 1] for a in range(groups)]

    first = density(0)
    for a in range(groups):
        stage[pl.ds(a, 8, stride=groups), :] = first[a]
        cols[me_n, pl.ds(0, 8), a * LANES:(a + 1) * LANES] = first[a]

    home = wide_of(z, y, 0) * unit
    own = pl.ds(pl.multiple_of(home + xl * unit, 8), unit)

    @pl.when(me_n == 0)
    def _():
        slab[own, :] = stage[pl.ds(0, unit), :]
        pl.semaphore_wait(barrier, always + n_x)
        for k in range(1, NX * n_narrow):
            xx, n = lax.rem(xl + k // n_narrow, NX), k % n_narrow
            pltpu.make_async_remote_copy(
                src_ref=stage.at[pl.ds(n * unit, unit)],
                dst_ref=slab.at[own],
                send_sem=x_send,
                recv_sem=x_recv.at[xl],
                device_id=dev(wide_of(z, y, xx), n),
                device_id_type=MESH,
            ).start()

    @pl.when(me_n != 0)
    def _():
        pl.semaphore_wait(barrier, always)

    for c in rests:
        c.wait()

    def other(g, _):
        start = pl.multiple_of(g * 8, 8)
        dens = density(start)
        for a in range(groups):
            cols[me_n, pl.ds(start, 8), a * LANES:(a + 1) * LANES] = dens[a]
        return 0

    lax.fori_loop(1, points // 8, other, 0)
    for k in range(1, n_narrow):
        pltpu.make_async_remote_copy(
            src_ref=cols.at[me_n],
            dst_ref=cols.at[me_n],
            send_sem=col_send,
            recv_sem=col_recv.at[me_n],
            device_id=dev(me_w, lax.rem(me_n + k, n_narrow)),
            device_id_type=MESH,
        ).start()

    def row_units(zz, yy):
        return pl.ds(pl.multiple_of(wide_of(zz, yy, 0) * unit, 16), pair_unit)

    def send(zz, to_z, to_y, send_sem, recv_sem):
        rows = slab.at[row_units(zz, y)]
        pltpu.make_async_remote_copy(
            src_ref=rows, dst_ref=rows, send_sem=send_sem, recv_sem=recv_sem,
            device_id=dev(wide_of(to_z, to_y, xl), me_n), device_id_type=MESH,
        ).start()

    def arrived(rows, sem):
        part = slab.at[pl.ds(0, rows)]
        pltpu.make_async_copy(part, part, sem).wait()

    def to_ys(zz):
        for i, dy in enumerate((1, 3, 2)):
            send(zz, z, shift_y(dy), y_send, y_recv.at[i])

    for src in range(NX):
        @pl.when(jnp.logical_or(me_n != 0, xl != src))
        def _():
            arrived(unit, x_recv.at[src])

    for dz in range(reach, 0, -1):
        send(z, shift_z(dz), y, z_send, z_recv.at[0, dz - 1])
        send(z, shift_z(-dz), y, z_send, z_recv.at[1, dz - 1])
    to_ys(z)
    for dz in Z_ORDER:
        for way in (0, 1):
            sign = 1 - 2 * way
            arrived(pair_unit, z_recv.at[way, dz - 1])
            if dz == reach:
                for k in range(reach - way, 0, -1):
                    send(shift_z(-sign * dz), shift_z(sign * k), y, z_send, far_recv.at[way, k - 1])
            to_ys(shift_z(-sign * dz))
    for k in range(1, reach + 1):
        for way in (0, 1):
            if k > reach - way:
                continue
            sign = 1 - 2 * way
            arrived(pair_unit, far_recv.at[way, k - 1])
            to_ys(shift_z(-sign * (reach + k)))

    def row_of(ref):
        return lambda c: jnp.broadcast_to(ref[pl.ds(c, 1), :], (8, LANES))

    energies = pick(row_of(ev), row_of(ec))
    weight = jnp.concatenate(
        [1.0 / (energies[2 * a + 1] - energies[2 * a]) for a in range(groups)], axis=1
    )[0:1]
    for k in range(1, n_narrow):
        n = lax.rem(me_n + k, n_narrow)
        pltpu.make_async_copy(cols.at[n], cols.at[n], col_recv.at[n]).wait()
    columns = jnp.concatenate([cols[n] for n in range(n_narrow)], axis=0) * weight
    left_hi = columns.astype(jnp.bfloat16)
    left_lo = (columns - left_hi.astype(jnp.float32)).astype(jnp.bfloat16)
    chi_load.wait()
    for i in range(3):
        arrived(nz * pair_unit, y_recv.at[i])

    def dot(x, t):
        return lax.dot_general(
            x, t, (((1,), (1,)), ((), ())), preferred_element_type=jnp.float32
        )

    slab_rows = out_ref.shape[1]
    step = 256
    for j in range(slab_rows // step):
        right = jnp.concatenate(
            [
                slab[pl.ds(j * step * groups + a, step, stride=groups), :]
                for a in range(groups)
            ],
            axis=1,
        )
        right_hi = right.astype(jnp.bfloat16)
        right_lo = (right - right_hi.astype(jnp.float32)).astype(jnp.bfloat16)
        at = slice(j * step, (j + 1) * step)
        out_ref[:, at] = chi[:, at] + (
            dot(left_hi, right_hi) + (dot(left_hi, right_lo) + dot(left_lo, right_hi))
        )

    @pl.when(me_n == 0)
    def _():
        arrived(n_x * unit, x_send)
    whole = cols.at[pl.ds(0, n_narrow - 1)]
    pltpu.make_async_copy(whole, whole, col_send).wait()
    arrived((4 * reach - 1) * pair_unit, z_send)
    arrived(nz * pair_unit * 3, y_send)


def shards(chi_in, val_orb, cond_orb, e_val, e_cond, pair_val, pair_cond):
    n_wide, n_narrow = lax.axis_size("wide"), lax.axis_size("narrow")
    points, bands = val_orb.shape
    g_dev, slab_rows = chi_in.shape
    pairs = pair_val.shape[1]
    groups = pairs // LANES
    nz = n_wide // (NY * NX)
    reach = nz // 4
    any_space = pl.BlockSpec(memory_space=pl.ANY)
    dma = pltpu.SemaphoreType.DMA
    return pl.pallas_call(
        functools.partial(kernel, n_wide, n_narrow, pairs, reach),
        out_shape=jax.ShapeDtypeStruct(chi_in.shape, jnp.float32),
        in_specs=[any_space] * 7,
        out_specs=pl.BlockSpec(memory_space=pltpu.VMEM),
        scratch_shapes=[
            pltpu.VMEM((1, pairs), jnp.int32),
            pltpu.VMEM((1, pairs), jnp.int32),
            pltpu.VMEM((bands // LANES, LANES), jnp.float32),
            pltpu.VMEM((bands // LANES, LANES), jnp.float32),
            pltpu.VMEM((points, bands), jnp.float32),
            pltpu.VMEM((points, bands), jnp.float32),
            pltpu.VMEM((g_dev, slab_rows), jnp.float32),
            pltpu.VMEM((8 * groups, LANES), jnp.float32),
            pltpu.VMEM((slab_rows * groups, LANES), jnp.float32),
            pltpu.VMEM((n_narrow, points, pairs), jnp.float32),
            dma((9,)),
            dma,
            dma((NX,)),
            dma,
            dma((n_narrow,)),
            dma,
            dma((2, reach)),
            dma((2, reach)),
            dma,
            dma((3,)),
        ],
        compiler_params=pltpu.CompilerParams(
            collective_id=0, has_side_effects=True, vmem_limit_bytes=60 << 20
        ),
        name="chi_slab",
    )(
        pair_val,
        pair_cond,
        e_val.reshape(bands // LANES, LANES),
        e_cond.reshape(bands // LANES, LANES),
        val_orb,
        cond_orb,
        chi_in,
    )


def solution(mesh):
    placed = (
        P("wide", "narrow"),
        P(("wide", "narrow"), None),
        P(("wide", "narrow"), None),
        P(),
        P(),
        P(),
        P(),
    )
    return jax.shard_map(
        shards, mesh=mesh, in_specs=placed, out_specs=P("wide", "narrow"), check_vma=False
    )
```

time: 924 us -> 61.3 us (0.07)
  waiting for transfers between devices: 882 us -> 0 us
  Pallas kernels: 0 us -> 59.4 us
  local copies, waits for them, and re-layouts: 16.3 us -> 1.72 us
  between operations: 13.5 us -> 0.01 us
    all_gather x1 -> x0, waiting for transfers between devices: 882 us -> none  [shards(): lax.all_gather(pieces[:, 0, :], 'wide', axis=0, tiled=True)]
    pallas_call x0 -> x1, Pallas kernels: none -> 59.4 us  [shards(): pl.pallas_call(functools.partial(kernel, n_wide, n_narrow, pairs, reach),...]
    gather x4 -> x0, local copies, waits for them, and re-layouts: 9.95 us -> none  [the longest x2 6.29 us: shards(): weight = 1.0 / (e_cond[pair_cond] - e_val[pair_val])]
  transfers between devices with their start and end apart: 1 -> 0, of which waited for: 1 -> 0; matrix products, arithmetic and copies ran while one was open for 1% -> 0% of each run, Pallas kernels for 0% -> 0%
where the time goes in v1:
time: 61.3 us; the launch traced here: 61.1 us
  Pallas kernels  59.4 us (97%)
  local copies, waits for them, and re-layouts  1.72 us (3%)
    pallas_call x1, Pallas kernels, shards(): pl.pallas_call(functools.partial(kernel, n_wide, n_narrow, pairs, reach),...  59.4 us
    unnamed x1, local copies, waits for them, and re-layouts  1.72 us

profile of v1, /device:TPU:6, one launch (start us, length us, event | category | flops | bytes accessed | tf_op | source)
XLA Modules:
  0.0 61.1 jit_solution(2456241756336209181)
XLA Ops:
  0.0 59.4 %chi_slab.1 = f32[160,512]{1,0:T(8,128)} custom-call(s32[1,512]{1,0:T(1,128)} %pv_ref.1, s32[1,512]{1,0:T(1,128)} %pc_ref.1, f32[32,128]{1,0:T(8,128)} %bitcast.2, f32[32,128]{1,0:T(8,128)} %bitcast.3, f32[40,4096]{1,0:T(8,128)} %val_ref.1, f32[40,4096]{1,0:T(8,128)} %cond_ref.1, f32[160,512]{1,0:T(8,128)} %chi_ref.1), custom_call_target="tpu_custom_call" | custom-call | tf_op jit(solution)/shard_map/chi_slab/pallas_call | solution.py:269
  59.4 1.7 %copy.9 = f32[160,512]{1,0:T(8,128)} copy(f32[160,512]{1,0:T(8,128)} %chi_slab.1) | data formatting | bytes 655360

commit v2 on v1

--- a/solution.py
+++ b/solution.py
@@ -12,14 +12,16 @@
 NY = 4
 NX = 2
 Z_ORDER = (1, 2, 3, 8, 4, 5, 6, 7)
+UNROLL = 16
+EARLY = 3
 
 
 def kernel(
     n_wide, n_narrow, pairs, reach,
     pv_ref, pc_ref, ev_ref, ec_ref, val_ref, cond_ref, chi_ref,
     out_ref,
-    pv, pc, ev, ec, vbuf, cbuf, chi, stage, slab, cols,
-    in_sems, x_send, x_recv, col_send, col_recv, z_send, z_recv, far_recv, y_send, y_recv,
+    pv, pc, ev, ec, vbuf, cbuf, chi, weights, stage, slab, cols,
+    permit, in_sems, x_send, x_recv, col_send, col_recv, z_send, z_recv, far_recv, y_send, y_recv,
 ):
     me_w = lax.axis_index("wide")
     me_n = lax.axis_index("narrow")
@@ -74,10 +76,11 @@
         greet(me_w, lax.rem(me_n + k, n_narrow))
     for dy in (1, 3, 2):
         greet(wide_of(z, shift_y(dy), xl), me_n)
-    for dz in range(1, reach + 1):
+    near = reach // 2
+    for dz in range(1, near + 1):
         greet(wide_of(shift_z(dz), y, xl), me_n)
         greet(wide_of(shift_z(-dz), y, xl), me_n)
-    always = (n_narrow - 1) + 3 + 2 * reach
+    always = (n_narrow - 1) + 3 + 2 * near
 
     for c in small:
         c.wait()
@@ -93,20 +96,23 @@
     chunks = vbuf.shape[1] // LANES
 
     def pick(load_v, load_c):
-        def body(c, acc):
-            rows_v, rows_c = load_v(c), load_c(c)
-            new = []
-            for a in range(groups):
-                for rows, (lo, hi), old in (
-                    (rows_v, idx_v[a], acc[2 * a]),
-                    (rows_c, idx_c[a], acc[2 * a + 1]),
-                ):
-                    got = jnp.take_along_axis(rows, lo, axis=1, mode="promise_in_bounds")
-                    new.append(jnp.where(hi == c, got, old))
-            return tuple(new)
+        def body(i, acc):
+            for u in range(UNROLL):
+                c = i * UNROLL + u
+                rows_v, rows_c = load_v(c), load_c(c)
+                new = []
+                for a in range(groups):
+                    for rows, (lo, hi), old in (
+                        (rows_v, idx_v[a], acc[2 * a]),
+                        (rows_c, idx_c[a], acc[2 * a + 1]),
+                    ):
+                        got = jnp.take_along_axis(rows, lo, axis=1, mode="promise_in_bounds")
+                        new.append(jnp.where(hi == c, got, old))
+                acc = tuple(new)
+            return acc
 
         zero = jnp.zeros((8, LANES), jnp.float32)
-        return lax.fori_loop(0, chunks, body, (zero,) * (2 * groups))
+        return lax.fori_loop(0, chunks // UNROLL, body, (zero,) * (2 * groups))
 
     def density(start):
         def load(ref):
@@ -121,6 +127,24 @@
     for a in range(groups):
         stage[pl.ds(a, 8, stride=groups), :] = first[a]
         cols[me_n, pl.ds(0, 8), a * LANES:(a + 1) * LANES] = first[a]
+
+    for c in rests:
+        c.wait()
+
+    def other(g, _):
+        start = pl.multiple_of(g * 8, 8)
+        dens = density(start)
+        for a in range(groups):
+            cols[me_n, pl.ds(start, 8), a * LANES:(a + 1) * LANES] = dens[a]
+        return 0
+
+    def row_of(ref):
+        return lambda c: jnp.broadcast_to(ref[pl.ds(c, 1), :], (8, LANES))
+
+    energies = pick(row_of(ev), row_of(ec))
+    for a in range(groups):
+        weights[:, a * LANES:(a + 1) * LANES] = 1.0 / (energies[2 * a + 1] - energies[2 * a])
+    lax.fori_loop(1, EARLY, other, 0)
 
     home = wide_of(z, y, 0) * unit
     own = pl.ds(pl.multiple_of(home + xl * unit, 8), unit)
@@ -144,17 +168,13 @@
     def _():
         pl.semaphore_wait(barrier, always)
 
-    for c in rests:
-        c.wait()
-
-    def other(g, _):
-        start = pl.multiple_of(g * 8, 8)
-        dens = density(start)
-        for a in range(groups):
-            cols[me_n, pl.ds(start, 8), a * LANES:(a + 1) * LANES] = dens[a]
-        return 0
-
-    lax.fori_loop(1, points // 8, other, 0)
+    for way in (0, 1):
+        to = shift_z((2 * way - 1) * near)
+        pl.semaphore_signal(
+            permit.at[way], inc=1, device_id=dev(wide_of(to, y, xl), me_n), device_id_type=MESH
+        )
+
+    lax.fori_loop(EARLY, points // 8, other, 0)
     for k in range(1, n_narrow):
         pltpu.make_async_remote_copy(
             src_ref=cols.at[me_n],
@@ -187,6 +207,9 @@
         @pl.when(jnp.logical_or(me_n != 0, xl != src))
         def _():
             arrived(unit, x_recv.at[src])
+
+    for way in (0, 1):
+        pl.semaphore_wait(permit.at[way], 1)
 
     for dz in range(reach, 0, -1):
         send(z, shift_z(dz), y, z_send, z_recv.at[0, dz - 1])
@@ -208,17 +231,10 @@
             arrived(pair_unit, far_recv.at[way, k - 1])
             to_ys(shift_z(-sign * (reach + k)))
 
-    def row_of(ref):
-        return lambda c: jnp.broadcast_to(ref[pl.ds(c, 1), :], (8, LANES))
-
-    energies = pick(row_of(ev), row_of(ec))
-    weight = jnp.concatenate(
-        [1.0 / (energies[2 * a + 1] - energies[2 * a]) for a in range(groups)], axis=1
-    )[0:1]
     for k in range(1, n_narrow):
         n = lax.rem(me_n + k, n_narrow)
         pltpu.make_async_copy(cols.at[n], cols.at[n], col_recv.at[n]).wait()
-    columns = jnp.concatenate([cols[n] for n in range(n_narrow)], axis=0) * weight
+    columns = jnp.concatenate([cols[n] for n in range(n_narrow)], axis=0) * weights[0:1, :]
     left_hi = columns.astype(jnp.bfloat16)
     left_lo = (columns - left_hi.astype(jnp.float32)).astype(jnp.bfloat16)
     chi_load.wait()
@@ -279,9 +295,11 @@
             pltpu.VMEM((points, bands), jnp.float32),
             pltpu.VMEM((points, bands), jnp.float32),
             pltpu.VMEM((g_dev, slab_rows), jnp.float32),
+            pltpu.VMEM((8, pairs), jnp.float32),
             pltpu.VMEM((8 * groups, LANES), jnp.float32),
             pltpu.VMEM((slab_rows * groups, LANES), jnp.float32),
             pltpu.VMEM((n_narrow, points, pairs), jnp.float32),
+            pltpu.SemaphoreType.REGULAR((2,)),
             dma((9,)),
             dma,
             dma((NX,)),

time: 61.3 us -> 51.2 us (0.84)
  Pallas kernels: 59.4 us -> 49.3 us
    pallas_call x1, Pallas kernels: 59.4 us -> 49.3 us  [shards(): pl.pallas_call(functools.partial(kernel, n_wide, n_narrow, pairs, reach),...]
where the time goes in v2:
time: 51.2 us; the launch traced here: 51 us
  Pallas kernels  49.3 us (96%)
  local copies, waits for them, and re-layouts  1.72 us (3%)
    pallas_call x1, Pallas kernels, shards(): pl.pallas_call(functools.partial(kernel, n_wide, n_narrow, pairs, reach),...  49.3 us
    unnamed x1, local copies, waits for them, and re-layouts  1.72 us

profile of v2, /device:TPU:6, one launch (start us, length us, event | category | flops | bytes accessed | tf_op | source)
XLA Modules:
  0.0 51.0 jit_solution(3009179241456636321)
XLA Ops:
  0.0 49.3 %chi_slab.1 = f32[160,512]{1,0:T(8,128)} custom-call(s32[1,512]{1,0:T(1,128)} %pv_ref.1, s32[1,512]{1,0:T(1,128)} %pc_ref.1, f32[32,128]{1,0:T(8,128)} %bitcast.2, f32[32,128]{1,0:T(8,128)} %bitcast.3, f32[40,4096]{1,0:T(8,128)} %val_ref.1, f32[40,4096]{1,0:T(8,128)} %cond_ref.1, f32[160,512]{1,0:T(8,128)} %chi_ref.1), custom_call_target="tpu_custom_call" | custom-call | tf_op jit(solution)/shard_map/chi_slab/pallas_call | solution.py:285
  49.3 1.7 %copy.9 = f32[160,512]{1,0:T(8,128)} copy(f32[160,512]{1,0:T(8,128)} %chi_slab.1) | data formatting | bytes 655360

commit v3 on v2

--- a/solution.py
+++ b/solution.py
@@ -11,9 +11,13 @@
 LANES = 128
 NY = 4
 NX = 2
-Z_ORDER = (1, 2, 3, 8, 4, 5, 6, 7)
+TREE = {0: (8, 4, 3, 2, 1), 4: (7, 6, 5)}
+RELAY = 8
+ARRIVALS = (1, 2, 3, 4, 8, 5, 6, 7)
+Y_SHIFTS = (2, 1, 3)
+X_SHIFTS = (2, 1, 3, 0)
 UNROLL = 16
-EARLY = 3
+EARLY = 2
 
 
 def kernel(
@@ -21,7 +25,7 @@
     pv_ref, pc_ref, ev_ref, ec_ref, val_ref, cond_ref, chi_ref,
     out_ref,
     pv, pc, ev, ec, vbuf, cbuf, chi, weights, stage, slab, cols,
-    permit, in_sems, x_send, x_recv, col_send, col_recv, z_send, z_recv, far_recv, y_send, y_recv,
+    permit, in_sems, x_send, x_recv, col_send, col_recv, z_send, z_recv, y_send, y_recv, pair_recv,
 ):
     me_w = lax.axis_index("wide")
     me_n = lax.axis_index("narrow")
@@ -74,13 +78,15 @@
             greet(wide_of(z, y, src), 0)
     for k in range(1, n_narrow):
         greet(me_w, lax.rem(me_n + k, n_narrow))
-    for dy in (1, 3, 2):
+    for dy in Y_SHIFTS:
         greet(wide_of(z, shift_y(dy), xl), me_n)
+    for dy in X_SHIFTS:
+        greet(wide_of(z, shift_y(dy), 1 - xl), me_n)
     near = reach // 2
     for dz in range(1, near + 1):
         greet(wide_of(shift_z(dz), y, xl), me_n)
         greet(wide_of(shift_z(-dz), y, xl), me_n)
-    always = (n_narrow - 1) + 3 + 2 * near
+    always = (n_narrow - 1) + len(Y_SHIFTS) + len(X_SHIFTS) + 2 * near
 
     for c in small:
         c.wait()
@@ -138,12 +144,6 @@
             cols[me_n, pl.ds(start, 8), a * LANES:(a + 1) * LANES] = dens[a]
         return 0
 
-    def row_of(ref):
-        return lambda c: jnp.broadcast_to(ref[pl.ds(c, 1), :], (8, LANES))
-
-    energies = pick(row_of(ev), row_of(ec))
-    for a in range(groups):
-        weights[:, a * LANES:(a + 1) * LANES] = 1.0 / (energies[2 * a + 1] - energies[2 * a])
     lax.fori_loop(1, EARLY, other, 0)
 
     home = wide_of(z, y, 0) * unit
@@ -188,11 +188,11 @@
     def row_units(zz, yy):
         return pl.ds(pl.multiple_of(wide_of(zz, yy, 0) * unit, 16), pair_unit)
 
-    def send(zz, to_z, to_y, send_sem, recv_sem):
+    def send(zz, to_z, to_y, to_x, send_sem, recv_sem):
         rows = slab.at[row_units(zz, y)]
         pltpu.make_async_remote_copy(
             src_ref=rows, dst_ref=rows, send_sem=send_sem, recv_sem=recv_sem,
-            device_id=dev(wide_of(to_z, to_y, xl), me_n), device_id_type=MESH,
+            device_id=dev(wide_of(to_z, to_y, to_x), me_n), device_id_type=MESH,
         ).start()
 
     def arrived(rows, sem):
@@ -200,8 +200,21 @@
         pltpu.make_async_copy(part, part, sem).wait()
 
     def to_ys(zz):
-        for i, dy in enumerate((1, 3, 2)):
-            send(zz, z, shift_y(dy), y_send, y_recv.at[i])
+        for i, dy in enumerate(Y_SHIFTS):
+            send(zz, z, shift_y(dy), xl, y_send, y_recv.at[i])
+
+    def to_xs(zz):
+        for i, dy in enumerate(X_SHIFTS):
+            send(zz, z, shift_y(dy), 1 - xl, y_send, pair_recv.at[i])
+
+    def far_loop(do):
+        for i in range(reach // NX):
+            at = reach + 1 + NX * i + xl
+            do(0, at)
+            if i < reach // NX - 1:
+                do(1, at)
+            else:
+                pl.when(xl == 0)(functools.partial(do, 1, at))
 
     for src in range(NX):
         @pl.when(jnp.logical_or(me_n != 0, xl != src))
@@ -211,25 +224,46 @@
     for way in (0, 1):
         pl.semaphore_wait(permit.at[way], 1)
 
-    for dz in range(reach, 0, -1):
-        send(z, shift_z(dz), y, z_send, z_recv.at[0, dz - 1])
-        send(z, shift_z(-dz), y, z_send, z_recv.at[1, dz - 1])
+    def z_sends(way, at):
+        sign = 1 - 2 * way
+        for to in TREE[at]:
+            send(
+                shift_z(-sign * at), shift_z(sign * (to - at)), y, xl,
+                z_send, z_recv.at[way, to - 1],
+            )
+
+    def relay(way, to):
+        sign = 1 - 2 * way
+        send(
+            shift_z(-sign * RELAY), shift_z(sign * (to - RELAY)), y, xl,
+            z_send, z_recv.at[way, to - 1],
+        )
+
+    def far_arrive(way, at):
+        arrived(pair_unit, z_recv.at[way, at - 1])
+        zz = shift_z((2 * way - 1) * at)
+        to_xs(zz)
+        to_ys(zz)
+
+    for way in (0, 1):
+        z_sends(way, 0)
     to_ys(z)
-    for dz in Z_ORDER:
+    def row_of(ref):
+        return lambda c: jnp.broadcast_to(ref[pl.ds(c, 1), :], (8, LANES))
+
+    energies = pick(row_of(ev), row_of(ec))
+    for a in range(groups):
+        weights[:, a * LANES:(a + 1) * LANES] = 1.0 / (energies[2 * a + 1] - energies[2 * a])
+    for at in ARRIVALS:
         for way in (0, 1):
-            sign = 1 - 2 * way
-            arrived(pair_unit, z_recv.at[way, dz - 1])
-            if dz == reach:
-                for k in range(reach - way, 0, -1):
-                    send(shift_z(-sign * dz), shift_z(sign * k), y, z_send, far_recv.at[way, k - 1])
-            to_ys(shift_z(-sign * dz))
-    for k in range(1, reach + 1):
+            arrived(pair_unit, z_recv.at[way, at - 1])
+            if at in TREE:
+                z_sends(way, at)
+        if at == RELAY:
+            far_loop(relay)
         for way in (0, 1):
-            if k > reach - way:
-                continue
-            sign = 1 - 2 * way
-            arrived(pair_unit, far_recv.at[way, k - 1])
-            to_ys(shift_z(-sign * (reach + k)))
+            to_ys(shift_z((2 * way - 1) * at))
+    far_loop(far_arrive)
 
     for k in range(1, n_narrow):
         n = lax.rem(me_n + k, n_narrow)
@@ -238,8 +272,16 @@
     left_hi = columns.astype(jnp.bfloat16)
     left_lo = (columns - left_hi.astype(jnp.float32)).astype(jnp.bfloat16)
     chi_load.wait()
-    for i in range(3):
-        arrived(nz * pair_unit, y_recv.at[i])
+    n_near = 1 + 2 * reach
+    n_far = (reach, reach - 1)
+    for c in range(NX):
+        @pl.when(xl == c)
+        def _():
+            for i in range(len(Y_SHIFTS)):
+                arrived((n_near + n_far[c]) * pair_unit, y_recv.at[i])
+            for i in range(len(X_SHIFTS)):
+                arrived(n_far[1 - c] * pair_unit, pair_recv.at[i])
+
 
     def dot(x, t):
         return lax.dot_general(
@@ -268,8 +310,12 @@
         arrived(n_x * unit, x_send)
     whole = cols.at[pl.ds(0, n_narrow - 1)]
     pltpu.make_async_copy(whole, whole, col_send).wait()
-    arrived((4 * reach - 1) * pair_unit, z_send)
-    arrived(nz * pair_unit * 3, y_send)
+    for c in range(NX):
+        @pl.when(xl == c)
+        def _():
+            n_y, n_x_shifts = len(Y_SHIFTS), len(X_SHIFTS)
+            arrived((n_near - 1 + n_far[c]) * pair_unit, z_send)
+            arrived((n_y * n_near + (n_y + n_x_shifts) * n_far[c]) * pair_unit, y_send)
 
 
 def shards(chi_in, val_orb, cond_orb, e_val, e_cond, pair_val, pair_cond):
@@ -306,10 +352,10 @@
             dma,
             dma((n_narrow,)),
             dma,
-            dma((2, reach)),
-            dma((2, reach)),
+            dma((2, 2 * reach)),
             dma,
-            dma((3,)),
+            dma((len(Y_SHIFTS),)),
+            dma((len(X_SHIFTS),)),
         ],
         compiler_params=pltpu.CompilerParams(
             collective_id=0, has_side_effects=True, vmem_limit_bytes=60 << 20

time: 51.2 us -> 48.1 us (0.939); the launches traced: 51 us -> 47.3 us
  Pallas kernels: 49.3 us -> 45.5 us
    pallas_call x1, Pallas kernels: 49.3 us -> 45.5 us  [shards(): pl.pallas_call(functools.partial(kernel, n_wide, n_narrow, pairs, reach),...]
where the time goes in v3:
time: 48.1 us; the launch traced here: 47.3 us
  Pallas kernels  45.5 us (95%)
  local copies, waits for them, and re-layouts  1.72 us (4%)
    pallas_call x1, Pallas kernels, shards(): pl.pallas_call(functools.partial(kernel, n_wide, n_narrow, pairs, reach),...  45.5 us
    unnamed x1, local copies, waits for them, and re-layouts  1.72 us

profile of v3, /device:TPU:6, one launch (start us, length us, event | category | flops | bytes accessed | tf_op | source)
XLA Modules:
  0.0 47.3 jit_solution(1711832806567479873)
XLA Ops:
  0.0 45.5 %chi_slab.1 = f32[160,512]{1,0:T(8,128)} custom-call(s32[1,512]{1,0:T(1,128)} %pv_ref.1, s32[1,512]{1,0:T(1,128)} %pc_ref.1, f32[32,128]{1,0:T(8,128)} %bitcast.2, f32[32,128]{1,0:T(8,128)} %bitcast.3, f32[40,4096]{1,0:T(8,128)} %val_ref.1, f32[40,4096]{1,0:T(8,128)} %cond_ref.1, f32[160,512]{1,0:T(8,128)} %chi_ref.1), custom_call_target="tpu_custom_call" | custom-call | tf_op jit(solution)/shard_map/chi_slab/pallas_call | solution.py:331
  45.5 1.7 %copy.9 = f32[160,512]{1,0:T(8,128)} copy(f32[160,512]{1,0:T(8,128)} %chi_slab.1) | data formatting | bytes 655360

commit v4 on v3

--- a/solution.py
+++ b/solution.py
@@ -64,7 +64,7 @@
         for i, (s, d) in enumerate([(val_ref, vbuf), (cond_ref, cbuf)])
     ]
     chi_load = pltpu.make_async_copy(chi_ref, chi, in_sems.at[8])
-    for c in small + heads + rests + [chi_load]:
+    for c in heads + small + rests + [chi_load]:
         c.start()
 
     barrier = pltpu.get_barrier_semaphore()
@@ -72,6 +72,10 @@
     def greet(w, n):
         pl.semaphore_signal(barrier, inc=1, device_id=dev(w, n), device_id_type=MESH)
 
+    near = reach // 2
+    for dz in range(near, 0, -1):
+        greet(wide_of(shift_z(dz), y, xl), me_n)
+        greet(wide_of(shift_z(-dz), y, xl), me_n)
     for src in range(NX):
         @pl.when(jnp.logical_or(me_n != 0, xl != src))
         def _():
@@ -82,10 +86,6 @@
         greet(wide_of(z, shift_y(dy), xl), me_n)
     for dy in X_SHIFTS:
         greet(wide_of(z, shift_y(dy), 1 - xl), me_n)
-    near = reach // 2
-    for dz in range(1, near + 1):
-        greet(wide_of(shift_z(dz), y, xl), me_n)
-        greet(wide_of(shift_z(-dz), y, xl), me_n)
     always = (n_narrow - 1) + len(Y_SHIFTS) + len(X_SHIFTS) + 2 * near
 
     for c in small:
@@ -207,8 +207,8 @@
         for i, dy in enumerate(X_SHIFTS):
             send(zz, z, shift_y(dy), 1 - xl, y_send, pair_recv.at[i])
 
-    def far_loop(do):
-        for i in range(reach // NX):
+    def far_loop(do, order):
+        for i in order(range(reach // NX)):
             at = reach + 1 + NX * i + xl
             do(0, at)
             if i < reach // NX - 1:
@@ -260,10 +260,10 @@
             if at in TREE:
                 z_sends(way, at)
         if at == RELAY:
-            far_loop(relay)
+            far_loop(relay, reversed)
         for way in (0, 1):
             to_ys(shift_z((2 * way - 1) * at))
-    far_loop(far_arrive)
+    far_loop(far_arrive, iter)
 
     for k in range(1, n_narrow):
         n = lax.rem(me_n + k, n_narrow)

time: 48.1 us -> 47.5 us (0.988)
  Pallas kernels: 45.5 us -> 44.9 us
    pallas_call x1, Pallas kernels: 45.5 us -> 44.9 us  [shards(): pl.pallas_call(functools.partial(kernel, n_wide, n_narrow, pairs, reach),...]
where the time goes in v4:
time: 47.5 us; the launch traced here: 46.7 us
  Pallas kernels  44.9 us (95%)
  local copies, waits for them, and re-layouts  1.72 us (4%)
    pallas_call x1, Pallas kernels, shards(): pl.pallas_call(functools.partial(kernel, n_wide, n_narrow, pairs, reach),...  44.9 us
    unnamed x1, local copies, waits for them, and re-layouts  1.72 us

profile of v4, /device:TPU:6, one launch (start us, length us, event | category | flops | bytes accessed | tf_op | source)
XLA Modules:
  0.0 46.7 jit_solution(5874472999045332382)
XLA Ops:
  0.0 44.9 %chi_slab.1 = f32[160,512]{1,0:T(8,128)} custom-call(s32[1,512]{1,0:T(1,128)} %pv_ref.1, s32[1,512]{1,0:T(1,128)} %pc_ref.1, f32[32,128]{1,0:T(8,128)} %bitcast.2, f32[32,128]{1,0:T(8,128)} %bitcast.3, f32[40,4096]{1,0:T(8,128)} %val_ref.1, f32[40,4096]{1,0:T(8,128)} %cond_ref.1, f32[160,512]{1,0:T(8,128)} %chi_ref.1), custom_call_target="tpu_custom_call" | custom-call | tf_op jit(solution)/shard_map/chi_slab/pallas_call | solution.py:331
  44.9 1.7 %copy.9 = f32[160,512]{1,0:T(8,128)} copy(f32[160,512]{1,0:T(8,128)} %chi_slab.1) | data formatting | bytes 655360

commit v5 on v4

--- a/solution.py
+++ b/solution.py
@@ -11,9 +11,9 @@
 LANES = 128
 NY = 4
 NX = 2
-TREE = {0: (8, 4, 3, 2, 1), 4: (7, 6, 5)}
+TREE = {0: (8, 4, 2, 1), 2: (3,), 4: (6, 5), 6: (7,)}
 RELAY = 8
-ARRIVALS = (1, 2, 3, 4, 8, 5, 6, 7)
+ARRIVALS = (1, 2, 4, 3, 8, 5, 6, 7)
 Y_SHIFTS = (2, 1, 3)
 X_SHIFTS = (2, 1, 3, 0)
 UNROLL = 16
@@ -342,8 +342,8 @@
             pltpu.VMEM((points, bands), jnp.float32),
             pltpu.VMEM((g_dev, slab_rows), jnp.float32),
             pltpu.VMEM((8, pairs), jnp.float32),
-            pltpu.VMEM((8 * groups, LANES), jnp.float32),
-            pltpu.VMEM((slab_rows * groups, LANES), jnp.float32),
+            pltpu.VMEM((8 * groups + 8, LANES), jnp.float32),
+            pltpu.VMEM((slab_rows * groups + 8, LANES), jnp.float32),
             pltpu.VMEM((n_narrow, points, pairs), jnp.float32),
             pltpu.SemaphoreType.REGULAR((2,)),
             dma((9,)),

time: 47.5 us -> 47.2 us (level)
  no operation moved by 1% of the time
where the time goes in v5:
time: 47.2 us; the launch traced here: 46.6 us
  Pallas kernels  44.9 us (95%)
  local copies, waits for them, and re-layouts  1.72 us (4%)
    pallas_call x1, Pallas kernels, shards(): pl.pallas_call(functools.partial(kernel, n_wide, n_narrow, pairs, reach),...  44.9 us
    unnamed x1, local copies, waits for them, and re-layouts  1.72 us

profile of v5, /device:TPU:6, one launch (start us, length us, event | category | flops | bytes accessed | tf_op | source)
XLA Modules:
  0.0 46.6 jit_solution(16700576033202338747)
XLA Ops:
  0.0 44.9 %chi_slab.1 = f32[160,512]{1,0:T(8,128)} custom-call(s32[1,512]{1,0:T(1,128)} %pv_ref.1, s32[1,512]{1,0:T(1,128)} %pc_ref.1, f32[32,128]{1,0:T(8,128)} %bitcast.2, f32[32,128]{1,0:T(8,128)} %bitcast.3, f32[40,4096]{1,0:T(8,128)} %val_ref.1, f32[40,4096]{1,0:T(8,128)} %cond_ref.1, f32[160,512]{1,0:T(8,128)} %chi_ref.1), custom_call_target="tpu_custom_call" | custom-call | tf_op jit(solution)/shard_map/chi_slab/pallas_call | solution.py:331
  44.9 1.7 %copy.9 = f32[160,512]{1,0:T(8,128)} copy(f32[160,512]{1,0:T(8,128)} %chi_slab.1) | data formatting | bytes 655360
